TPU v7x, 32 devices: a whole 2x2x4 slice. The times are simulated.
32 devices in a mesh: dp: 2 (over x), context: 4 (over y, core), tensor: 4 (over z).
Axes of the slice: x: 2, y: 2, z: 4, core: 2. Of those that a mesh axis runs over, the one named last changes fastest.
Arguments:
- tokens: bfloat16 [8192, 4096], P(('dp', 'context'), 'tensor'), parts along dimension 0, may hold values from -6 to 6
- norm_gain: float32 [4096], replicated, may hold values from 0.5 to 1.5
- in_weight: bfloat16 [3, 4096, 4096], P(None, 'context', 'tensor'), may hold values from -0.09375 to 0.09375
- short_taps: float32 [3, 7, 4096], P(None, None, 'tensor'), may hold values from -2.5 to 2.5
- long_filter: float32 [4096, 128], P('tensor'), may hold values from -0.5 to 0.5
- skip_bias: float32 [4096], P('tensor'), may hold values from -3 to 3
- segment_ids: int32 [8192], P('dp'), parts along dimension 0, may hold values from 0 to 31, never falling along the last dimension, each value on 1 to 256 neighbouring positions
Outputs:
- mixed: bfloat16 [8192, 4096], P(('dp', 'context'), 'tensor'), parts along dimension 0
There are 2 independent parts, one for each index of `dp`. A program takes and returns all parts, laid end to end along the dimension named above; an argument that names none is the same for every part. Nothing has to cross between parts.
Inputs may be any that keep to these rules, and one draw needn't show every extreme that they name: `segment_ids`: never falling, starting at 0; every document has 1 to 256 tokens and some has exactly 256.
All inputs are finite; a program needn't handle non-finite values.
Results may differ from a plain program's by a relative error of at most 0.0086.
Values may be sent and summed in bfloat16 or wider, within the bound.
A program may use at most 128 MiB of HBM per device.

v0:
```python
import jax
import jax.numpy as jnp
from jax import lax
from jax.sharding import PartitionSpec as P


def shifted_2(shard, axis, by):
    size = lax.axis_size(axis)
    pairs = [(i, i + by) for i in range(size) if 0 <= i + by < size]
    return lax.ppermute(shard, axis, pairs)


def distances(segment_ids):
    count = segment_ids.shape[0]
    places = jnp.arange(count, dtype=jnp.int32)
    earlier = jnp.concatenate([segment_ids[:1] - 1, segment_ids[:-1]])
    starts = jnp.where(segment_ids != earlier, places, jnp.zeros_like(places))
    first = lax.cummax(starts, axis=0)
    return places - first


def featurize(extended, short_taps, dist_rows, count):
    lead = short_taps.shape[1] - 1
    total = jnp.zeros((3, count, extended.shape[2]), jnp.float32)
    for lag in range(short_taps.shape[1]):
        shifted = extended[:, lead - lag : lead - lag + count].astype(jnp.float32)
        valid = (dist_rows >= lag).astype(jnp.float32)
        total = total + short_taps[:, lag][:, None, :] * shifted * valid[None, :, None]
    return total


def add_rows(normed, piece):
    return jnp.dot(normed, piece, preferred_element_type=jnp.float32)


def per_device(tokens, norm_gain, in_weight, short_taps, long_filter, skip_bias, segment_ids):
    rows = tokens.shape[0]
    local_channels = in_weight.shape[2]
    reach = long_filter.shape[1] - 1
    lead = short_taps.shape[1] - 1
    deep = reach + lead
    first = lax.axis_index("context") * rows
    dist_full = jnp.concatenate([jnp.full((deep,), -1, jnp.int32), distances(segment_ids)])
    whole = lax.all_gather(tokens, "tensor", axis=1, tiled=True)
    wide = whole.astype(jnp.float32)
    scale = lax.rsqrt(jnp.mean(wide * wide, axis=1, keepdims=True) + 1e-06)
    normed = (wide * scale * norm_gain[None, :]).astype(jnp.bfloat16)

    def add_one(piece):
        return add_rows(normed, piece)

    branches = [
        add_one(lax.all_gather(in_weight[g], "context", axis=0, tiled=True)) for g in range(3)
    ]
    proj = jnp.stack(list(branches)).astype(jnp.bfloat16)
    dist_local = lax.dynamic_slice_in_dim(dist_full, first + deep, rows, 0)
    received = shifted_2(proj[:, rows - lead :], "context", 1)
    extended = jnp.concatenate([received, proj], axis=1)
    feat = featurize(extended, short_taps, dist_local, rows)
    inner = (feat[1] * feat[2]).astype(jnp.bfloat16)
    earlier_inner = shifted_2(inner[rows - reach :], "context", 1)
    inner_all = jnp.concatenate([earlier_inner, inner], axis=0)
    gate_rows = feat[0]
    filt = jnp.transpose(long_filter)
    group = 16

    def turn(block, acc):
        for offset in range(group):
            lag = block * group + offset
            source = lax.dynamic_slice_in_dim(inner_all, reach - lag, rows, 0).astype(jnp.float32)
            weight = lax.dynamic_slice_in_dim(filt, lag, 1, 0)
            valid = (dist_local >= lag).astype(jnp.float32)
            acc = acc + weight * source * valid[:, None]
        return acc

    conv = lax.fori_loop(
        0, filt.shape[0] // group, turn, jnp.zeros((rows, local_channels), jnp.float32)
    )
    inner_local = inner_all[reach:].astype(jnp.float32)
    return (gate_rows * (conv + skip_bias[None, :] * inner_local)).astype(jnp.bfloat16)


def solution(mesh):
    placed = (
        P(("dp", "context"), "tensor"),
        P(),
        P(None, "context", "tensor"),
        P(None, None, "tensor"),
        P("tensor", None),
        P("tensor"),
        P("dp"),
    )
    return jax.shard_map(
        per_device,
        mesh=mesh,
        in_specs=placed,
        out_specs=P(("dp", "context"), "tensor"),
        check_vma=False,
    )
```

profile of v0, /device:TPU:0, one launch (start us, length us, event | category | flops | bytes accessed | tf_op | source)
XLA Modules:
  0.0 591.2 jit_solution(17138730986184587149)
XLA Ops:
  6.5 0.7 all-gather.8.cloned.1.call-update
  7.3 5.8 fusion.36
  13.2 0.7 all-gather.10.cloned.1.call-update
  13.9 0.5 all-gather.14.cloned.1.call-update
  14.5 0.6 slice.83
  15.7 0.1 select_bitcast_fusion
  15.7 0.3 reduce-window.9
  16.0 0.1 slice.105
  16.1 0.1 reduce-window.12
  16.2 0.1 slice_reduce_fusion
  16.3 0.1 bitcast_subtract_fusion
  16.4 0.1 compare_convert_fusion.22
  16.4 0.1 fusion.37
  16.6 144.7 %all-gather.8.cloned.1.call-done = bf16[1024,4096]{1,0:T(8,128)(2,1)} async-done(((bf16[1024,1024]{1,0:T(8,128)(2,1)}), bf16[1024,4096]{1,0:T(8,128)(2,1)}) %all-gather.8.cloned.1.call-update) | async-done | bytes 8388624 | tf_op jit(solution)/shard_map/all_gather | solution.py:44
  161.3 5.1 fusion.15
  166.4 53.0 %all-gather.12.cloned.1.call-done = bf16[1,4096,1024]{2,1,0:T(8,128)(2,1)} async-done(((bf16[1,1024,1024]{2,1,0:T(8,128)(2,1)}), bf16[1,4096,1024]{2,1,0:T(8,128)(2,1)}) %all-gather.12.cloned.1.call-update) | async-done | bytes 8388624 | tf_op jit(solution)/shard_map/all_gather | solution.py:53
  219.4 13.8 %convert_bitcast_fusion.1 = bf16[1,1024,1024]{2,1,0:T(8,128)(2,1)S(1)} fusion(bf16[1,4096,1024]{2,1,0:T(8,128)(2,1)} %all-gather.12.cloned.1.call-done, bf16[1024,4096]{1,0:T(8,128)(2,1)} %all-gather.8.cloned.1.call-done, f32[4096]{0:T(1024)S(1)} %copy-done.9, f32[1024]{0:T(1024)S(1)} %add_rsqrt_fusion), kind=kOutput, calls=%fused_computation.69 | convolution fusion | flops 8607760384 | bytes 18894848 | tf_op jit(solution)/shard_map/dot_general | solution.py:33
  233.1 46.1 %all-gather.10.cloned.1.call-done = bf16[1,4096,1024]{2,1,0:T(8,128)(2,1)} async-done(((bf16[1,1024,1024]{2,1,0:T(8,128)(2,1)}), bf16[1,4096,1024]{2,1,0:T(8,128)(2,1)}) %all-gather.10.cloned.1.call-update) | async-done | bytes 8388624 | tf_op jit(solution)/shard_map/all_gather | solution.py:53
  279.3 14.8 %convert_bitcast_fusion.2 = bf16[1,1024,1024]{2,1,0:T(8,128)(2,1)} fusion(bf16[1,4096,1024]{2,1,0:T(8,128)(2,1)} %all-gather.10.cloned.1.call-done, bf16[1024,4096]{1,0:T(8,128)(2,1)} %all-gather.8.cloned.1.call-done, f32[4096]{0:T(1024)S(1)} %copy-done.9, f32[1024]{0:T(1024)S(1)} %add_rsqrt_fusion), kind=kOutput, calls=%fused_computation.70 | convolution fusion | flops 8607760384 | bytes 18894848 | tf_op jit(solution)/shard_map/dot_general | solution.py:33
  294.0 44.9 %all-gather.14.cloned.1.call-done = bf16[1,4096,1024]{2,1,0:T(8,128)(2,1)} async-done(((bf16[1,1024,1024]{2,1,0:T(8,128)(2,1)}), bf16[1,4096,1024]{2,1,0:T(8,128)(2,1)}) %all-gather.14.cloned.1.call-update) | async-done | bytes 8388624 | tf_op jit(solution)/shard_map/all_gather | solution.py:53
  339.0 13.9 %convert_bitcast_fusion = bf16[1,1024,1024]{2,1,0:T(8,128)(2,1)S(1)} fusion(bf16[1,4096,1024]{2,1,0:T(8,128)(2,1)} %all-gather.14.cloned.1.call-done, bf16[1024,4096]{1,0:T(8,128)(2,1)} %all-gather.8.cloned.1.call-done, f32[4096]{0:T(1024)S(1)} %copy-done.9, f32[1024]{0:T(1024)S(1)} %add_rsqrt_fusion), kind=kOutput, calls=%fused_computation.68 | convolution fusion | flops 8607760384 | bytes 18894848 | tf_op jit(solution)/shard_map/dot_general | solution.py:33
  352.9 0.8 pad_maximum_fusion
  353.7 0.5 copy-done.3
  354.3 2.4 collective-permute-start
  356.7 0.2 copy.9
  356.9 0.4 collective-permute-done
  357.3 4.3 maximum_maximum_fusion
  361.6 14.4 %multiply_add_fusion = f32[3,1024,1024]{2,1,0:T(8,128)S(1)} fusion(bf16[3,1030,1024]{2,1,0:T(8,128)(2,1)S(1)} %maximum_maximum_fusion, f32[1024]{0:T(1024)S(1)} %get-tuple-element.286, f32[3,1024]{1,0:T(4,128)S(1)} %get-tuple-element.291, f32[1024]{0:T(1024)S(1)} %get-tuple-element.287, f32[3,1024]{1,0:T(4,128)S(1)} %get-tuple-element.292, ...), kind=kLoop, calls=%fused_computation.53 | loop fusion | flops 91226112 | bytes 56737792 | tf_op jit(solution)/shard_map/add | solution.py:28
  376.0 0.7 fusion.24
  376.8 0.1 slice_bitcast_fusion.1
  376.9 2.5 collective-permute-start.1
  379.4 0.7 fusion.38
  380.1 0.4 collective-permute-done.1
  380.5 0.6 pad_maximum_fusion.1
  381.1 194.3 %while.17 = (s32[]{:T(128)}, f32[1024,1024]{1,0:T(8,128)}, f32[128,1024]{1,0:T(8,128)S(1)}, bf16[1151,1024]{1,0:T(8,128)(2,1)S(1)}, s32[1024]{0:T(1024)S(1)}, /*...) while((s32[]{:T(128)}, f32[1024,1024]{1,0:T(8,128)}, ...), condition=%wide.region_4.5_spmd.clone, body=%wide.region_3.4_spmd.clone.sunk | while | flops 68190336 | bytes 42276828 | solution.py:76
  381.3 0.1 constant_dynamic-slice_fusion.17
  381.6 23.1 %fusion.40 = f32[1024,1024]{1,0:T(8,128)} fusion(f32[1024,1024]{1,0:T(8,128)} %get-tuple-element.433, f32[1024]{0:T(1024)S(1)} %get-tuple-element.360, bf16[1151,1024]{1,0:T(8,128)(2,1)S(1)} %get-tuple-element.475, s32[]{:T(128)S(6)} %select_n.426, f32[1024]{0:T(1024)S(1)} %bitcast.103, f32[1024]{0:T(1024)S(1)} %get-tuple-element.362, ...), kind=kLoop, calls=%fused_computation.15.clone.1 | loop fusion | flops 68157440 | bytes 42074176 | tf_op jit(solution)/shard_map/while/body/eval_jaxpr/add | solution.py:73
  404.7 0.1 constant_dynamic-slice_fusion.17
  405.0 24.1 %fusion.40 = f32[1024,1024]{1,0:T(8,128)} fusion(f32[1024,1024]{1,0:T(8,128)} %get-tuple-element.433, f32[1024]{0:T(1024)S(1)} %get-tuple-element.360, bf16[1151,1024]{1,0:T(8,128)(2,1)S(1)} %get-tuple-element.475, s32[]{:T(128)S(6)} %select_n.426, f32[1024]{0:T(1024)S(1)} %bitcast.103, f32[1024]{0:T(1024)S(1)} %get-tuple-element.362, ...), kind=kLoop, calls=%fused_computation.15.clone.1 | loop fusion | flops 68157440 | bytes 42074176 | tf_op jit(solution)/shard_map/while/body/eval_jaxpr/add | solution.py:73
  429.1 0.1 constant_dynamic-slice_fusion.17
  429.3 24.1 %fusion.40 = f32[1024,1024]{1,0:T(8,128)} fusion(f32[1024,1024]{1,0:T(8,128)} %get-tuple-element.433, f32[1024]{0:T(1024)S(1)} %get-tuple-element.360, bf16[1151,1024]{1,0:T(8,128)(2,1)S(1)} %get-tuple-element.475, s32[]{:T(128)S(6)} %select_n.426, f32[1024]{0:T(1024)S(1)} %bitcast.103, f32[1024]{0:T(1024)S(1)} %get-tuple-element.362, ...), kind=kLoop, calls=%fused_computation.15.clone.1 | loop fusion | flops 68157440 | bytes 42074176 | tf_op jit(solution)/shard_map/while/body/eval_jaxpr/add | solution.py:73
  453.7 24.1 %fusion.40 = f32[1024,1024]{1,0:T(8,128)} fusion(f32[1024,1024]{1,0:T(8,128)} %get-tuple-element.433, f32[1024]{0:T(1024)S(1)} %get-tuple-element.360, bf16[1151,1024]{1,0:T(8,128)(2,1)S(1)} %get-tuple-element.475, s32[]{:T(128)S(6)} %select_n.426, f32[1024]{0:T(1024)S(1)} %bitcast.103, f32[1024]{0:T(1024)S(1)} %get-tuple-element.362, ...), kind=kLoop, calls=%fused_computation.15.clone.1 | loop fusion | flops 68157440 | bytes 42074176 | tf_op jit(solution)/shard_map/while/body/eval_jaxpr/add | solution.py:73
  478.1 24.1 %fusion.40 = f32[1024,1024]{1,0:T(8,128)} fusion(f32[1024,1024]{1,0:T(8,128)} %get-tuple-element.433, f32[1024]{0:T(1024)S(1)} %get-tuple-element.360, bf16[1151,1024]{1,0:T(8,128)(2,1)S(1)} %get-tuple-element.475, s32[]{:T(128)S(6)} %select_n.426, f32[1024]{0:T(1024)S(1)} %bitcast.103, f32[1024]{0:T(1024)S(1)} %get-tuple-element.362, ...), kind=kLoop, calls=%fused_computation.15.clone.1 | loop fusion | flops 68157440 | bytes 42074176 | tf_op jit(solution)/shard_map/while/body/eval_jaxpr/add | solution.py:73
  502.5 24.1 %fusion.40 = f32[1024,1024]{1,0:T(8,128)} fusion(f32[1024,1024]{1,0:T(8,128)} %get-tuple-element.433, f32[1024]{0:T(1024)S(1)} %get-tuple-element.360, bf16[1151,1024]{1,0:T(8,128)(2,1)S(1)} %get-tuple-element.475, s32[]{:T(128)S(6)} %select_n.426, f32[1024]{0:T(1024)S(1)} %bitcast.103, f32[1024]{0:T(1024)S(1)} %get-tuple-element.362, ...), kind=kLoop, calls=%fused_computation.15.clone.1 | loop fusion | flops 68157440 | bytes 42074176 | tf_op jit(solution)/shard_map/while/body/eval_jaxpr/add | solution.py:73
  526.9 24.1 %fusion.40 = f32[1024,1024]{1,0:T(8,128)} fusion(f32[1024,1024]{1,0:T(8,128)} %get-tuple-element.433, f32[1024]{0:T(1024)S(1)} %get-tuple-element.360, bf16[1151,1024]{1,0:T(8,128)(2,1)S(1)} %get-tuple-element.475, s32[]{:T(128)S(6)} %select_n.426, f32[1024]{0:T(1024)S(1)} %bitcast.103, f32[1024]{0:T(1024)S(1)} %get-tuple-element.362, ...), kind=kLoop, calls=%fused_computation.15.clone.1 | loop fusion | flops 68157440 | bytes 42074176 | tf_op jit(solution)/shard_map/while/body/eval_jaxpr/add | solution.py:73
  551.0 0.1 constant_dynamic-slice_fusion.17
  551.3 24.1 %fusion.40 = f32[1024,1024]{1,0:T(8,128)} fusion(f32[1024,1024]{1,0:T(8,128)} %get-tuple-element.433, f32[1024]{0:T(1024)S(1)} %get-tuple-element.360, bf16[1151,1024]{1,0:T(8,128)(2,1)S(1)} %get-tuple-element.475, s32[]{:T(128)S(6)} %select_n.426, f32[1024]{0:T(1024)S(1)} %bitcast.103, f32[1024]{0:T(1024)S(1)} %get-tuple-element.362, ...), kind=kLoop, calls=%fused_computation.15.clone.1 | loop fusion | flops 68157440 | bytes 42074176 | tf_op jit(solution)/shard_map/while/body/eval_jaxpr/add | solution.py:73
  575.4 9.3 %fusion.26 = bf16[1024,1024]{1,0:T(8,128)(2,1)} fusion(f32[3,1024,1024]{2,1,0:T(8,128)} %copy-done, f32[1024,1024]{1,0:T(8,128)} %get-tuple-element.212, f32[1024]{0:T(1024)S(1)} %copy-done.8), kind=kLoop, calls=%fused_computation.66 | loop fusion | flops 7340032 | bytes 18878464 | tf_op jit(solution)/shard_map/convert_element_type | solution.py:80
  (44 shorter events, 0.8 us)
Async XLA Ops:
  6.5 154.8 %all-gather.8.cloned.1.call-start = ((), (), s32[]{:S(2)}) async-start(), calls=%async_computation | async-start | bytes 10485760 | tf_op jit(solution)/shard_map/all_gather | solution.py:44
  7.3 212.1 %all-gather.12.cloned.1.call-start = ((), (), s32[]{:S(2)}) async-start(), calls=%async_computation.2 | async-start | bytes 10485760 | tf_op jit(solution)/shard_map/all_gather | solution.py:53
  13.1 1.4 copy-start.7
  13.1 3.3 copy-start.6
  13.1 266.1 %all-gather.10.cloned.1.call-start = ((), (), s32[]{:S(2)}) async-start(), calls=%async_computation.1 | async-start | bytes 10485760 | tf_op jit(solution)/shard_map/all_gather | solution.py:53
  13.9 325.1 %all-gather.14.cloned.1.call-start = ((), (), s32[]{:S(2)}) async-start(), calls=%async_computation.3 | async-start | bytes 10485760 | tf_op jit(solution)/shard_map/all_gather | solution.py:53
  16.6 202.8 %copy-start.9 = (f32[4096]{0:T(1024)S(1)}, f32[4096]{0:T(1024)}, u32[]{:S(2)}) copy-start(f32[4096]{0:T(1024)} %param.10) | copy-start | bytes 49156
  339.0 13.9 %copy-start.1 = (bf16[1,1024,1024]{2,1,0:T(8,128)(2,1)S(1)}, bf16[1,1024,1024]{2,1,0:T(8,128)(2,1)}, u32[]{:S(2)}) copy-start(bf16[1,1024,1024]{2,1,0:T(8,128)(2,1)} %convert_bitcast_fusion.2) | copy-start | bytes 6291460
  352.9 1.3 copy-start.3
  352.9 3.8 copy-start.5
  354.3 3.0 collective-permute-start
  356.9 4.7 copy-start.2
  356.9 4.7 copy-start.4
  376.0 5.1 copy-start
  376.9 3.7 collective-permute-start.1
  381.1 194.3 %copy-start.8 = (f32[1024]{0:T(1024)S(1)}, f32[1024]{0:T(1024)}, u32[]{:S(2)}) copy-start(f32[1024]{0:T(1024)} %param.14) | copy-start | bytes 12292
Sparse Core Ops, SparseCore 0:
  8.9 152.3 all-gather.7
  162.9 56.4 all-gather.11
  220.9 58.2 all-gather.9
  280.7 58.2 all-gather.13
where the time goes:
time: 595 us; the launch traced here: 591 us
  waiting for transfers between devices  291 us (49%)
  other arithmetic  229 us (38%)
  matrix products  42.4 us (7%)
  between operations  14 us (2%)
  local copies, waits for them, and re-layouts  8 us (1%)
    add x8, other arithmetic, turn(): acc = acc + weight * source * valid[:, None]  192 us
    all_gather x1, waiting for transfers between devices, per_device(): whole = lax.all_gather(tokens, 'tensor', axis=1, tiled=True)  145 us
    all_gather x3, waiting for transfers between devices, per_device(): lax.all_gather(in_weight[g], 'context', axis=0, tiled=True)  144 us
    dot_general x3, matrix products, add_rows(): return jnp.dot(normed, piece, preferred_element_type=jnp.float32)  42.4 us
    add x1, other arithmetic, featurize(): total + short_taps[:, lag][:, None, :] * shifted * valid[None, :, None]  14.4 us
  transfers between devices with their start and end apart: 6, of which 6 were waited for; matrix products, arithmetic and copies ran while one was open for 7% of the time, Pallas kernels for 0%

commit v1 on v0

v1 whole, which is shorter than its diff:
```python
import functools
import math

import jax
import jax.numpy as jnp
import numpy as np
from jax import lax
from jax.experimental import pallas as pl
from jax.experimental.pallas import tpu as pltpu
from jax.sharding import PartitionSpec as P

MESH = pl.DeviceIdType.MESH
PIECES = 8
HALO = 144
BLOCK = 128
POINTS = 256


def gather_kernel(nt, nc, x_in, w_in, gain, out, xbuf, wbuf, normed, loc, xs, xr, ys, yr, ps, pr, cs, cr, os_, or_, hs, hr):
    d = lax.axis_index("dp")
    i = lax.axis_index("context")
    t = lax.axis_index("tensor")
    y, c = i // 2, i % 2
    ny = nc // 2
    rows = x_in.shape[0] // PIECES
    deep = w_in.shape[1]
    half = deep // 2
    sib = (d, i + 1 - 2 * c, t)
    peer = (1 - d, i, t)

    mine_x = pltpu.make_async_copy(x_in, xbuf.at[t], loc.at[0])
    mine_w = pltpu.make_async_copy(w_in, wbuf.at[:, pl.ds(i * deep, deep), :], loc.at[1])
    mine_x.start()
    mine_w.start()

    bar = pltpu.get_barrier_semaphore()

    def greet(dev):
        pl.semaphore_signal(bar, inc=1, device_id=dev, device_id_type=MESH)

    greet(sib)
    greet(peer)
    peers = jnp.int32(2)
    for cond, dev in (
        (t > 0, (d, i, t - 1)),
        (t < nt - 1, (d, i, t + 1)),
        (y > 0, (d, i - 2, t)),
        (y < ny - 1, (d, i + 2, t)),
        ((c == 0) & (i > 0), (d, i - 1, t)),
        ((c == 1) & (i < nc - 1), (d, i + 1, t)),
    ):
        peers = peers + cond.astype(jnp.int32)

        @pl.when(cond)
        def _():
            greet(dev)

    pl.semaphore_wait(bar, peers)

    def spot(r):
        return pl.multiple_of(lax.rem(r + PIECES - 2, PIECES) * rows, rows)

    def xcopy(side, hop, r, block, first):
        place = pl.ds(spot(r), rows)
        dst = xbuf.at[block, place, :]
        src = x_in.at[place, :] if first else dst
        to = (d, i, t + 1) if side == 0 else (d, i, t - 1)
        return pltpu.make_async_remote_copy(src, dst, xs.at[side, hop, r], xr.at[side, hop, r], device_id=to, device_id_type=MESH)

    def x_sends(side, hop):
        return (t < nt - 1) & (t - hop >= 0) if side == 0 else (t > 0) & (t + hop < nt)

    def x_takes(side, hop):
        return t - 1 - hop >= 0 if side == 0 else t + 1 + hop < nt

    def x_sent(side, hop):
        return t - hop if side == 0 else t + hop

    def x_taken(side, hop):
        return t - 1 - hop if side == 0 else t + 1 + hop

    def when(cond, f):
        pl.when(cond)(f)

    def wspan(block, part):
        return pl.ds(pl.multiple_of(block * deep + part * half, half), half)

    def ycopy(side, hop, g, yb, first):
        place = wspan(yb * 2 + c, d)
        dst = wbuf.at[g, place, :]
        src = w_in.at[g, pl.ds(pl.multiple_of(d * half, half), half), :] if first else dst
        to = (d, i + 2, t) if side == 0 else (d, i - 2, t)
        return pltpu.make_async_remote_copy(src, dst, ys.at[side, hop, g], yr.at[side, hop, g], device_id=to, device_id_type=MESH)

    def y_sends(side, hop):
        return (y < ny - 1) & (y - hop >= 0) if side == 0 else (y > 0) & (y + hop < ny)

    def y_takes(side, hop):
        return y - 1 - hop >= 0 if side == 0 else y + 1 + hop < ny

    def y_sent(side, hop):
        return y - hop if side == 0 else y + hop

    def y_taken(side, hop):
        return y - 1 - hop if side == 0 else y + 1 + hop

    def pcopy(side, hop, g, yb, part):
        at = wbuf.at[g, wspan(yb * 2 + c, part), :]
        return pltpu.make_async_remote_copy(at, at, ps.at[side, hop, g], pr.at[side, hop, g], device_id=peer, device_id_type=MESH)

    def ccopy(side, hop, g, via, yb, core, part):
        at = wbuf.at[g, wspan(yb * 2 + core, part), :]
        return pltpu.make_async_remote_copy(at, at, cs.at[side, hop, g, via], cr.at[side, hop, g, via], device_id=sib, device_id_type=MESH)

    def ocopy(block):
        at = wbuf.at[:, pl.ds(pl.multiple_of(block * deep, deep), deep), :]
        return pltpu.make_async_remote_copy(w_in, at, os_, or_, device_id=sib, device_id_type=MESH)

    sides = (0, 1)

    for g in range(3):
        for side in sides:
            when(y_sends(side, 0), lambda: ycopy(side, 0, g, y, True).start())

    def start_own(r, carry):
        for side in sides:
            when(x_sends(side, 0), lambda: xcopy(side, 0, r, t, True).start())
        return carry

    lax.fori_loop(0, PIECES, start_own, 0)
    ocopy(i).start()

    def pass_x(r, carry):
        for hop in range(nt - 2):
            for side in sides:
                @pl.when(x_takes(side, hop))
                def _():
                    xcopy(side, hop, r, x_taken(side, hop), False).wait_recv()

                when(x_sends(side, hop + 1), lambda: xcopy(side, hop + 1, r, x_sent(side, hop + 1), False).start())
        return carry

    def pass_w(g):
        for hop in range(ny - 1):
            for side in sides:
                @pl.when(y_takes(side, hop))
                def _():
                    yb = y_taken(side, hop)
                    ycopy(side, hop, g, yb, False).wait_recv()
                    pcopy(side, hop, g, yb, d).start()
                    ccopy(side, hop, g, 0, yb, c, d).start()

                if hop + 1 < ny - 1:
                    when(y_sends(side, hop + 1), lambda: ycopy(side, hop + 1, g, y_sent(side, hop + 1), False).start())

    def pass_p(g):
        for hop in range(ny - 1):
            for side in sides:
                @pl.when(y_takes(side, hop))
                def _():
                    yb = y_taken(side, hop)
                    pcopy(side, hop, g, yb, 1 - d).wait_recv()
                    ccopy(side, hop, g, 1, yb, c, 1 - d).start()

    cuts = (2, 4, 6)
    at = 0
    for g in range(3):
        lax.fori_loop(at, cuts[g], pass_x, 0)
        at = cuts[g]
        pass_w(g)
        if g:
            pass_p(g - 1)
    lax.fori_loop(at, PIECES, pass_x, 0)
    pass_p(2)

    mine_x.wait()
    mine_w.wait()
    ocopy(sib[1]).wait_recv()
    for g in range(3):
        for hop in range(ny - 1):
            for side in sides:
                @pl.when(y_takes(side, hop))
                def _():
                    yb = y_taken(side, hop)
                    ccopy(side, hop, g, 0, yb, 1 - c, d).wait_recv()
                    ccopy(side, hop, g, 1, yb, 1 - c, 1 - d).wait_recv()

    wide = w_in.shape[2]
    tile = min(512, wide)
    feats = x_in.shape[1]

    def project(r):
        for side in sides:
            when(x_takes(side, nt - 2), lambda: xcopy(side, nt - 2, r, x_taken(side, nt - 2), False).wait_recv())
        place = pl.ds(spot(r), rows)
        total = jnp.zeros((rows, 1), jnp.float32)
        for k in range(nt):
            v = xbuf[k, place, :].astype(jnp.float32)
            total = total + jnp.sum(v * v, axis=1, keepdims=True)
        scale = lax.rsqrt(total * (1.0 / (feats * nt)) + 1e-06)
        for k in range(nt):
            v = xbuf[k, place, :].astype(jnp.float32)
            cols = pl.ds(k * feats, feats)
            normed[:, cols] = (v * scale * gain[:, cols]).astype(jnp.bfloat16)
        to = pl.ds(pl.multiple_of(HALO + spot(r), 16), rows)

        def one(n, carry):
            g = n // (wide // tile)
            cols = pl.ds(pl.multiple_of((n % (wide // tile)) * tile, tile), tile)
            out[g, to, cols] = jnp.dot(normed[...], wbuf[g, :, cols], preferred_element_type=jnp.float32).astype(jnp.bfloat16)
            return carry

        lax.fori_loop(0, 3 * (wide // tile), one, 0)

    def project_step(r, carry):
        project(r)
        return carry

    total_rows = rows * PIECES

    def hcopy():
        return pltpu.make_async_remote_copy(
            out.at[:, pl.ds(total_rows, HALO), :], out.at[:, pl.ds(0, HALO), :], hs, hr, device_id=(d, i + 1, t), device_id_type=MESH
        )

    @pl.when(i == 0)
    def _():
        out[:, 0:HALO, :] = jnp.zeros((3, HALO, wide), jnp.bfloat16)

    lax.fori_loop(0, 2, project_step, 0)
    when(i < nc - 1, lambda: hcopy().start())
    lax.fori_loop(2, PIECES, project_step, 0)

    def drain(r, carry):
        for hop in range(nt - 1):
            for side in sides:
                when(x_sends(side, hop), lambda: xcopy(side, hop, r, x_sent(side, hop), False).wait_send())
        return carry

    lax.fori_loop(0, PIECES, drain, 0)
    for g in range(3):
        for hop in range(ny - 1):
            for side in sides:
                when(y_sends(side, hop), lambda: ycopy(side, hop, g, y_sent(side, hop), False).wait_send())

                @pl.when(y_takes(side, hop))
                def _():
                    yb = y_taken(side, hop)
                    pcopy(side, hop, g, yb, d).wait_send()
                    ccopy(side, hop, g, 0, yb, c, d).wait_send()
                    ccopy(side, hop, g, 1, yb, c, 1 - d).wait_send()
    ocopy(i).wait_send()
    when(i < nc - 1, lambda: hcopy().wait_send())
    when(i > 0, lambda: hcopy().wait_recv())


def project_all(nt, nc, tokens, in_weight, gain):
    rows, feats = tokens.shape
    deep, wide = in_weight.shape[1:]
    ny = nc // 2
    dma = pltpu.SemaphoreType.DMA
    hops = max(ny - 1, 1)
    return pl.pallas_call(
        functools.partial(gather_kernel, nt, nc),
        out_shape=jax.ShapeDtypeStruct((3, HALO + rows, wide), jnp.bfloat16),
        in_specs=[pl.BlockSpec(memory_space=pl.ANY)] * 2 + [pl.BlockSpec(memory_space=pltpu.VMEM)],
        out_specs=pl.BlockSpec(memory_space=pltpu.VMEM),
        scratch_shapes=[
            pltpu.VMEM((nt, rows, feats), jnp.bfloat16),
            pltpu.VMEM((3, nc * deep, wide), jnp.bfloat16),
            pltpu.VMEM((rows // PIECES, nt * feats), jnp.bfloat16),
            dma((2,)),
            dma((2, nt - 1, PIECES)),
            dma((2, nt - 1, PIECES)),
            dma((2, hops, 3)),
            dma((2, hops, 3)),
            dma((2, hops, 3)),
            dma((2, hops, 3)),
            dma((2, hops, 3, 2)),
            dma((2, hops, 3, 2)),
            dma,
            dma,
            dma,
            dma,
        ],
        compiler_params=pltpu.CompilerParams(collective_id=0, has_side_effects=True, vmem_limit_bytes=52 << 20),
        name="gather_project",
    )(tokens, in_weight, gain)


def transforms():
    k = np.arange(POINTS // 2)[:, None]
    n = np.arange(POINTS)[None, :]
    angle = 2 * np.pi * ((k * n) % POINTS) / POINTS
    cos, sin = np.cos(angle), -np.sin(angle)
    sin[0] = np.where(np.arange(POINTS) % 2 == 0, 1.0, -1.0)
    forward = np.concatenate([cos, sin], axis=0)
    weight = np.full((POINTS, 1), 2.0 / POINTS)
    weight[0] = weight[POINTS // 2] = 1.0 / POINTS
    back = (forward * weight).T[BLOCK:]
    return forward.astype(np.float32), back.astype(np.float32)


def conv_kernel(bounds, proj, taps, spec, skip, dist, seg, fwd, back, out, inner, gate):
    blocks = inner.shape[0] // BLOCK
    ntaps = taps.shape[1]

    def featurize(b, carry):
        start = pl.multiple_of(b * BLOCK, BLOCK)
        near = dist[pl.ds(pl.multiple_of(start + 16, 16), BLOCK), :]
        sums = [None] * 3
        valid = [near >= lag for lag in range(ntaps)]
        for g in range(3):
            whole = proj[g, pl.ds(start, BLOCK + 16), :].astype(jnp.float32)
            total = None
            for lag in range(ntaps):
                term = taps[g, lag : lag + 1, :] * whole[16 - lag : 16 - lag + BLOCK]
                term = jnp.where(valid[lag], term, 0.0)
                total = term if total is None else total + term
            sums[g] = total
        inner[pl.ds(start, BLOCK), :] = (sums[1] * sums[2]).astype(jnp.bfloat16)
        gate[pl.ds(start, BLOCK), :] = sums[0]
        return carry

    lax.fori_loop(0, blocks, featurize, 0)
    f = fwd[...]
    w = back[...]
    hb = POINTS // 2

    def filter_block(b, carry):
        start = pl.multiple_of(b * BLOCK, BLOCK)
        window = inner[pl.ds(start, 2 * BLOCK), :].astype(jnp.float32)
        ids = seg[pl.ds(pl.multiple_of(start + 16, 16), 2 * BLOCK), :]
        mine = ids[BLOCK:]

        def one(s, acc):
            x = jnp.where(ids == s, window, 0.0).astype(jnp.bfloat16)
            z = jnp.dot(f, x, preferred_element_type=jnp.float32)
            a, bb = z[:hb], z[hb:]
            re = a * spec[0] - bb * spec[1]
            im = a * spec[1] + bb * spec[2]
            prod = jnp.concatenate([re, im], axis=0).astype(jnp.bfloat16)
            return jnp.where(mine == s, jnp.dot(w, prod, preferred_element_type=jnp.float32), acc)

        conv = lax.fori_loop(bounds[b], bounds[blocks + b] + 1, one, jnp.zeros((BLOCK, out.shape[1]), jnp.float32))
        here = pl.ds(pl.multiple_of(start + BLOCK, BLOCK), BLOCK)
        mixed = gate[here, :] * (conv + skip[...] * window[BLOCK:])
        out[pl.ds(start, BLOCK), :] = mixed.astype(jnp.bfloat16)
        return carry

    lax.fori_loop(0, blocks - 1, filter_block, 0)


def filter_gate(proj, taps, spec, skip, dist, seg, bounds, fwd, back):
    _, ext, wide = proj.shape
    rows = ext - HALO
    cols = 256
    whole = lambda shape: pl.BlockSpec(shape, lambda j, b: (0,) * len(shape))
    return pl.pallas_call(
        conv_kernel,
        grid_spec=pltpu.PrefetchScalarGridSpec(
            num_scalar_prefetch=1,
            grid=(wide // cols,),
            in_specs=[
                pl.BlockSpec((3, ext, cols), lambda j, b: (0, 0, j)),
                pl.BlockSpec((3, taps.shape[1], cols), lambda j, b: (0, 0, j)),
                pl.BlockSpec((3, POINTS // 2, cols), lambda j, b: (0, 0, j)),
                pl.BlockSpec((1, cols), lambda j, b: (0, j)),
                whole((ext, cols)),
                whole((ext, cols)),
                whole((POINTS, POINTS)),
                whole((BLOCK, POINTS)),
            ],
            out_specs=pl.BlockSpec((rows, cols), lambda j, b: (0, j)),
            scratch_shapes=[
                pltpu.VMEM((rows + BLOCK, cols), jnp.bfloat16),
                pltpu.VMEM((rows + BLOCK, cols), jnp.float32),
            ],
        ),
        out_shape=jax.ShapeDtypeStruct((rows, wide), jnp.bfloat16),
        compiler_params=pltpu.CompilerParams(vmem_limit_bytes=40 << 20),
        name="filter_gate",
    )(bounds, proj, taps, spec, skip, dist, seg, fwd, back)


def distances(segment_ids):
    count = segment_ids.shape[0]
    places = jnp.arange(count, dtype=jnp.int32)
    earlier = jnp.concatenate([segment_ids[:1] - 1, segment_ids[:-1]])
    starts = jnp.where(segment_ids != earlier, places, jnp.zeros_like(places))
    return places - lax.cummax(starts, axis=0)


def per_device(nt, nc, tokens, norm_gain, in_weight, short_taps, long_filter, skip_bias, segment_ids):
    rows = tokens.shape[0]
    first = lax.axis_index("context") * rows
    pad = jnp.full((HALO,), -1, jnp.int32)
    ids = lax.dynamic_slice_in_dim(jnp.concatenate([pad, segment_ids]), first, rows + HALO, 0)
    dist = lax.dynamic_slice_in_dim(jnp.concatenate([pad, distances(segment_ids)]), first, rows + HALO, 0)
    bounds = jnp.concatenate([ids[HALO::BLOCK], ids[HALO + BLOCK - 1 :: BLOCK]])
    spread = lambda v: jnp.broadcast_to(v[:, None], (rows + HALO, 256))
    forward, back = transforms()
    full = jnp.dot(forward[:, : long_filter.shape[1]], long_filter.T, precision=lax.Precision.HIGHEST)
    top = (jnp.arange(BLOCK) == 0)[:, None]
    re, im = full[:BLOCK], full[BLOCK:]
    spec = jnp.stack([re, jnp.where(top, 0.0, im), jnp.where(top, im, re)])
    last = jnp.zeros((1,), jnp.int32)
    n = rows // BLOCK
    bounds = jnp.concatenate([bounds[:n], last, bounds[n:]])
    proj = project_all(nt, nc, tokens, in_weight, norm_gain[None, :])
    return filter_gate(
        proj, short_taps, spec, skip_bias[None, :], spread(dist), spread(ids), bounds,
        jnp.asarray(forward, jnp.bfloat16), jnp.asarray(back, jnp.bfloat16),
    )


def solution(mesh):
    placed = (
        P(("dp", "context"), "tensor"),
        P(),
        P(None, "context", "tensor"),
        P(None, None, "tensor"),
        P("tensor", None),
        P("tensor"),
        P("dp"),
    )
    return jax.shard_map(
        functools.partial(per_device, mesh.shape["tensor"], mesh.shape["context"]),
        mesh=mesh,
        in_specs=placed,
        out_specs=P(("dp", "context"), "tensor"),
        check_vma=False,
    )
```

time: 595 us -> 247 us (0.42)
  waiting for transfers between devices: 291 us -> 0 us
  Pallas kernels: 0 us -> 234 us
  other arithmetic: 229 us -> 1.68 us
  matrix products: 42.4 us -> 1.9 us
  between operations: 14 us -> 0.76 us
    all_gather x4 -> x0, waiting for transfers between devices: 289 us -> none  [the longest x1 145 us: per_device(): whole = lax.all_gather(tokens, 'tensor', axis=1, tiled=True)]
    pallas_call x0 -> x2, Pallas kernels: none -> 234 us  [the longest x1 182 us: project_all(): pl.pallas_call(functools.partial(gather_kernel, nt, nc), out_shape=jax.Sh...]
    add x9 -> x0, other arithmetic: 207 us -> none  [the longest x8 192 us: turn(): acc = acc + weight * source * valid[:, None]]
    dot_general x3 -> x1, matrix products: 42.4 us -> 1.9 us  [per_device(): jnp.dot(forward[:, :long_filter.shape[1]], long_filter.T, precision=lax.P...]
    convert_element_type x13 -> x0, other arithmetic: 11.2 us -> none  [the longest x1 9.25 us: per_device(): (gate_rows * (conv + skip_bias[None, :] * inner_local)).astype(jnp.bfloat16)]
  transfers between devices with their start and end apart: 6 -> 0, of which waited for: 6 -> 0; matrix products, arithmetic and copies ran while one was open for 7% -> 0% of each run, Pallas kernels for 0% -> 0%
where the time goes in v1:
time: 247 us; the launch traced here: 245 us
  Pallas kernels  234 us (95%)
  local copies, waits for them, and re-layouts  6.17 us (2%)
    pallas_call x1, Pallas kernels, project_all(): pl.pallas_call(functools.partial(gather_kernel, nt, nc), out_shape=jax.Sh...  182 us
    pallas_call x1, Pallas kernels, filter_gate(): pl.pallas_call(conv_kernel, grid_spec=pltpu.PrefetchScalarGridSpec(num_sc...  51.8 us

profile of v1, /device:TPU:0, one launch (start us, length us, event | category | flops | bytes accessed | tf_op | source)
XLA Modules:
  0.0 244.5 jit_solution(3628974787303203947)
XLA Ops:
  0.0 0.0 copy-start
  0.0 1.3 slice.29
  1.9 0.9 select_bitcast_fusion.2
  2.8 0.3 reduce-window.9
  3.1 0.1 slice.35
  3.2 0.1 reduce-window.12
  3.2 0.1 slice_reduce_fusion
  3.3 0.1 bitcast_subtract_fusion
  3.4 0.8 pad_dynamic-slice_fusion
  4.2 0.1 slice.26
  4.3 0.1 slice.25
  4.4 0.1 pad_add_fusion.bounds
  4.5 0.0 copy-done
  4.5 1.9 fusion
  6.4 0.1 select_bitcast_fusion.1
  6.5 0.2 pad_maximum_fusion.spec
  6.7 0.0 copy-start.5
  6.7 0.2 broadcast_in_dim.49.seg
  6.9 0.2 broadcast_in_dim.48.dist
  7.1 0.3 copy-done.5
  7.4 0.0 copy-start.2
  7.4 0.0 copy-start.3
  7.4 0.0 copy-start.4
  7.4 0.0 copy-start.6
  7.4 182.2 %gather_project.1.proj = bf16[3,1168,1024]{2,1,0:T(8,128)(2,1)} custom-call(bf16[1024,1024]{1,0:T(8,128)(2,1)} %x_in.1, bf16[3,1024,1024]{2,1,0:T(8,128)(2,1)} %w_in.1, f32[1,4096]{1,0:T(1,128)S(1)} %bitcast.15), custom_call_target="tpu_custom_call" | custom-call | tf_op jit(solution)/shard_map/gather_project/pallas_call | solution.py:263
  189.6 0.0 copy-done.2
  189.6 0.0 copy-done.3
  189.6 0.0 copy-done.4
  189.6 0.0 copy-done.6
  189.7 0.0 copy-start.1
  189.7 3.0 %copy-done.1 = bf16[3,1168,1024]{2,1,0:T(8,128)(2,1)S(1)} copy-done((bf16[3,1168,1024]{2,1,0:T(8,128)(2,1)S(1)}, bf16[3,1168,1024]{2,1,0:T(8,128)(2,1)}, u32[]{:S(2)}) %copy-start.1) | copy-done | bytes 7176216
  192.7 51.8 %filter_gate.1 = bf16[1024,1024]{1,0:T(8,128)(2,1)} custom-call(s32[17]{0:T(128)S(1)} %pad_add_fusion.bounds, bf16[3,1168,1024]{2,1,0:T(8,128)(2,1)S(1)} %copy-done.1, f32[3,7,1024]{2,1,0:T(8,128)S(1)} %copy-done.3, f32[3,128,1024]{2,1,0:T(8,128)S(1)} %pad_maximum_fusion.spec, f32[1,1024]{1,0:T(1,128)S(1)} %bitcast.16, ...), custom_call_target="tpu_custom_call" | custom-call | tf_op jit(solution)/shard_map/filter_gate/pallas_call | solution.py:359
  (1 shorter events, 0.0 us)
Async XLA Ops:
  0.0 4.5 %copy-start = (f32[1024,128]{1,0:T(8,128)S(1)}, f32[1024,128]{1,0:T(8,128)}, u32[]{:S(2)}) copy-start(f32[1024,128]{1,0:T(8,128)} %param.14) | copy-start | bytes 1572868
  6.7 0.7 copy-start.5
  7.4 182.2 %copy-start.2 = (bf16[256,256]{1,0:T(8,128)(2,1)S(1)}, bf16[256,256]{1,0:T(8,128)(2,1)}, u32[]{:S(2)}) copy-start(bf16[256,256]{1,0:T(8,128)(2,1)} %constant.32.clone.fwd) | copy-start | bytes 393220
  7.4 182.2 %copy-start.3 = (f32[3,7,1024]{2,1,0:T(8,128)S(1)}, f32[3,7,1024]{2,1,0:T(8,128)}, u32[]{:S(2)}) copy-start(f32[3,7,1024]{2,1,0:T(8,128)} %taps.1) | copy-start | bytes 258052
  7.4 182.2 %copy-start.4 = (bf16[128,256]{1,0:T(8,128)(2,1)S(1)}, bf16[128,256]{1,0:T(8,128)(2,1)}, u32[]{:S(2)}) copy-start(bf16[128,256]{1,0:T(8,128)(2,1)} %constant.33.clone.back) | copy-start | bytes 196612
  7.4 182.2 %copy-start.6 = (f32[1024]{0:T(1024)S(1)}, f32[1024]{0:T(1024)}, u32[]{:S(2)}) copy-start(f32[1024]{0:T(1024)} %param.15) | copy-start | bytes 12292
  189.7 3.0 %copy-start.1 = (bf16[3,1168,1024]{2,1,0:T(8,128)(2,1)S(1)}, bf16[3,1168,1024]{2,1,0:T(8,128)(2,1)}, u32[]{:S(2)}) copy-start(bf16[3,1168,1024]{2,1,0:T(8,128)(2,1)} %gather_project.1.proj) | copy-start | bytes 21528580

commit v2 on v1

--- a/solution.py
+++ b/solution.py
@@ -16,7 +16,7 @@
 POINTS = 256
 
 
-def gather_kernel(nt, nc, x_in, w_in, gain, out, xbuf, wbuf, normed, loc, xs, xr, ys, yr, ps, pr, cs, cr, os_, or_, hs, hr):
+def gather_kernel(nt, nc, x_in, w_in, gain, taps, dist, inner, gate, xbuf, wbuf, normed, out, strip, loc, xs, xr, ys, yr, ps, pr, cs, cr, os_, or_, hs, hr):
     d = lax.axis_index("dp")
     i = lax.axis_index("context")
     t = lax.axis_index("tensor")
@@ -130,14 +130,14 @@
     lax.fori_loop(0, PIECES, start_own, 0)
     ocopy(i).start()
 
-    def pass_x(r, carry):
-        for hop in range(nt - 2):
-            for side in sides:
-                @pl.when(x_takes(side, hop))
-                def _():
-                    xcopy(side, hop, r, x_taken(side, hop), False).wait_recv()
-
-                when(x_sends(side, hop + 1), lambda: xcopy(side, hop + 1, r, x_sent(side, hop + 1), False).start())
+    def pass_x(step, carry):
+        hop, r = step // PIECES, step % PIECES
+        for side in sides:
+            @pl.when(x_takes(side, hop))
+            def _():
+                xcopy(side, hop, r, x_taken(side, hop), False).wait_recv()
+
+            when(x_sends(side, hop + 1), lambda: xcopy(side, hop + 1, r, x_sent(side, hop + 1), False).start())
         return carry
 
     def pass_w(g):
@@ -162,7 +162,8 @@
                     pcopy(side, hop, g, yb, 1 - d).wait_recv()
                     ccopy(side, hop, g, 1, yb, c, 1 - d).start()
 
-    cuts = (2, 4, 6)
+    steps = (nt - 2) * PIECES
+    cuts = (steps // 4, steps // 2, 3 * steps // 4)
     at = 0
     for g in range(3):
         lax.fori_loop(at, cuts[g], pass_x, 0)
@@ -170,7 +171,7 @@
         pass_w(g)
         if g:
             pass_p(g - 1)
-    lax.fori_loop(at, PIECES, pass_x, 0)
+    lax.fori_loop(at, steps, pass_x, 0)
     pass_p(2)
 
     mine_x.wait()
@@ -212,8 +213,37 @@
 
         lax.fori_loop(0, 3 * (wide // tile), one, 0)
 
+    ntaps = taps.shape[1]
+
+    def featurize(start):
+        start = pl.multiple_of(start, BLOCK)
+        at = pl.ds(start, BLOCK)
+
+        def column(n, carry):
+            cols = pl.ds(pl.multiple_of(n * 128, 128), 128)
+            near = dist[pl.ds(pl.multiple_of(start + 16, 16), BLOCK), :]
+            sums = [None] * 3
+            for g in range(3):
+                strip[g] = out[g, pl.ds(start, BLOCK + 16), cols].astype(jnp.float32)
+            for lag in range(ntaps):
+                valid = near >= lag
+                for g in range(3):
+                    term = taps[g, lag : lag + 1, cols] * strip[g, 16 - lag : 16 - lag + BLOCK, :]
+                    term = jnp.where(valid, term, 0.0)
+                    sums[g] = term if lag == 0 else sums[g] + term
+            inner[at, cols] = (sums[1] * sums[2]).astype(jnp.bfloat16)
+            gate[at, cols] = sums[0]
+            return carry
+
+        lax.fori_loop(0, wide // 128, column, 0)
+
     def project_step(r, carry):
         project(r)
+        return carry
+
+    def both(r, carry):
+        project(r)
+        featurize(BLOCK + spot(r))
         return carry
 
     total_rows = rows * PIECES
@@ -229,7 +259,14 @@
 
     lax.fori_loop(0, 2, project_step, 0)
     when(i < nc - 1, lambda: hcopy().start())
-    lax.fori_loop(2, PIECES, project_step, 0)
+    featurize(BLOCK + (PIECES - 1) * rows)
+    lax.fori_loop(2, 4, project_step, 0)
+    when(i > 0, lambda: hcopy().wait_recv())
+    featurize(0)
+    featurize(BLOCK)
+    featurize(BLOCK + rows)
+    lax.fori_loop(4, PIECES, both, 0)
+    featurize(BLOCK + (PIECES - 2) * rows)
 
     def drain(r, carry):
         for hop in range(nt - 1):
@@ -251,10 +288,9 @@
                     ccopy(side, hop, g, 1, yb, c, 1 - d).wait_send()
     ocopy(i).wait_send()
     when(i < nc - 1, lambda: hcopy().wait_send())
-    when(i > 0, lambda: hcopy().wait_recv())
-
-
-def project_all(nt, nc, tokens, in_weight, gain):
+
+
+def project_all(nt, nc, tokens, in_weight, gain, taps, dist):
     rows, feats = tokens.shape
     deep, wide = in_weight.shape[1:]
     ny = nc // 2
@@ -262,13 +298,18 @@
     hops = max(ny - 1, 1)
     return pl.pallas_call(
         functools.partial(gather_kernel, nt, nc),
-        out_shape=jax.ShapeDtypeStruct((3, HALO + rows, wide), jnp.bfloat16),
-        in_specs=[pl.BlockSpec(memory_space=pl.ANY)] * 2 + [pl.BlockSpec(memory_space=pltpu.VMEM)],
-        out_specs=pl.BlockSpec(memory_space=pltpu.VMEM),
+        out_shape=(
+            jax.ShapeDtypeStruct((BLOCK + rows, wide), jnp.bfloat16),
+            jax.ShapeDtypeStruct((BLOCK + rows, wide), jnp.float32),
+        ),
+        in_specs=[pl.BlockSpec(memory_space=pl.ANY)] * 2 + [pl.BlockSpec(memory_space=pltpu.VMEM)] * 3,
+        out_specs=(pl.BlockSpec(memory_space=pltpu.VMEM),) * 2,
         scratch_shapes=[
             pltpu.VMEM((nt, rows, feats), jnp.bfloat16),
             pltpu.VMEM((3, nc * deep, wide), jnp.bfloat16),
             pltpu.VMEM((rows // PIECES, nt * feats), jnp.bfloat16),
+            pltpu.VMEM((3, HALO + rows, wide), jnp.bfloat16),
+            pltpu.VMEM((3, BLOCK + 16, 128), jnp.float32),
             dma((2,)),
             dma((2, nt - 1, PIECES)),
             dma((2, nt - 1, PIECES)),
@@ -283,9 +324,9 @@
             dma,
             dma,
         ],
-        compiler_params=pltpu.CompilerParams(collective_id=0, has_side_effects=True, vmem_limit_bytes=52 << 20),
+        compiler_params=pltpu.CompilerParams(collective_id=0, has_side_effects=True, vmem_limit_bytes=56 << 20),
         name="gather_project",
-    )(tokens, in_weight, gain)
+    )(tokens, in_weight, gain, taps, dist)
 
 
 def transforms():
@@ -301,28 +342,17 @@
     return forward.astype(np.float32), back.astype(np.float32)
 
 
-def conv_kernel(bounds, proj, taps, spec, skip, dist, seg, fwd, back, out, inner, gate):
+def conv_kernel(bounds, inner, gate, filt, skip, seg, wave, fwd, back, out, spec):
     blocks = inner.shape[0] // BLOCK
-    ntaps = taps.shape[1]
-
-    def featurize(b, carry):
-        start = pl.multiple_of(b * BLOCK, BLOCK)
-        near = dist[pl.ds(pl.multiple_of(start + 16, 16), BLOCK), :]
-        sums = [None] * 3
-        valid = [near >= lag for lag in range(ntaps)]
-        for g in range(3):
-            whole = proj[g, pl.ds(start, BLOCK + 16), :].astype(jnp.float32)
-            total = None
-            for lag in range(ntaps):
-                term = taps[g, lag : lag + 1, :] * whole[16 - lag : 16 - lag + BLOCK]
-                term = jnp.where(valid[lag], term, 0.0)
-                total = term if total is None else total + term
-            sums[g] = total
-        inner[pl.ds(start, BLOCK), :] = (sums[1] * sums[2]).astype(jnp.bfloat16)
-        gate[pl.ds(start, BLOCK), :] = sums[0]
-        return carry
-
-    lax.fori_loop(0, blocks, featurize, 0)
+    wide = out.shape[1]
+    full = lax.dot_general(
+        wave[...], filt[...], (((1,), (1,)), ((), ())), precision=lax.Precision.HIGHEST, preferred_element_type=jnp.float32
+    )
+    re0, im0 = full[:BLOCK], full[BLOCK:]
+    top = lax.broadcasted_iota(jnp.int32, re0.shape, 0) == 0
+    spec[0] = re0
+    spec[1] = jnp.where(top, 0.0, im0)
+    spec[2] = jnp.where(top, im0, re0)
     f = fwd[...]
     w = back[...]
     hb = POINTS // 2
@@ -331,6 +361,7 @@
         start = pl.multiple_of(b * BLOCK, BLOCK)
         window = inner[pl.ds(start, 2 * BLOCK), :].astype(jnp.float32)
         ids = seg[pl.ds(pl.multiple_of(start + 16, 16), 2 * BLOCK), :]
+        ids = jnp.concatenate([ids] * (wide // 128), axis=1)
         mine = ids[BLOCK:]
 
         def one(s, acc):
@@ -351,36 +382,34 @@
     lax.fori_loop(0, blocks - 1, filter_block, 0)
 
 
-def filter_gate(proj, taps, spec, skip, dist, seg, bounds, fwd, back):
-    _, ext, wide = proj.shape
-    rows = ext - HALO
-    cols = 256
-    whole = lambda shape: pl.BlockSpec(shape, lambda j, b: (0,) * len(shape))
+def filter_gate(inner, gate, filt, skip, seg, bounds, wave, fwd, back):
+    ext, wide = inner.shape
+    rows = ext - BLOCK
+    cols = min(512, wide)
+    column = lambda n: pl.BlockSpec((n, cols), lambda j, b: (0, j))
+    whole = lambda v: pl.BlockSpec(v.shape, lambda j, b: (0,) * v.ndim)
     return pl.pallas_call(
         conv_kernel,
         grid_spec=pltpu.PrefetchScalarGridSpec(
             num_scalar_prefetch=1,
             grid=(wide // cols,),
             in_specs=[
-                pl.BlockSpec((3, ext, cols), lambda j, b: (0, 0, j)),
-                pl.BlockSpec((3, taps.shape[1], cols), lambda j, b: (0, 0, j)),
-                pl.BlockSpec((3, POINTS // 2, cols), lambda j, b: (0, 0, j)),
-                pl.BlockSpec((1, cols), lambda j, b: (0, j)),
-                whole((ext, cols)),
-                whole((ext, cols)),
-                whole((POINTS, POINTS)),
-                whole((BLOCK, POINTS)),
+                column(ext),
+                column(ext),
+                pl.BlockSpec((cols, filt.shape[1]), lambda j, b: (j, 0)),
+                column(1),
+                whole(seg),
+                whole(wave),
+                whole(fwd),
+                whole(back),
             ],
-            out_specs=pl.BlockSpec((rows, cols), lambda j, b: (0, j)),
-            scratch_shapes=[
-                pltpu.VMEM((rows + BLOCK, cols), jnp.bfloat16),
-                pltpu.VMEM((rows + BLOCK, cols), jnp.float32),
-            ],
+            out_specs=column(rows),
+            scratch_shapes=[pltpu.VMEM((3, BLOCK, cols), jnp.float32)],
         ),
         out_shape=jax.ShapeDtypeStruct((rows, wide), jnp.bfloat16),
         compiler_params=pltpu.CompilerParams(vmem_limit_bytes=40 << 20),
         name="filter_gate",
-    )(bounds, proj, taps, spec, skip, dist, seg, fwd, back)
+    )(bounds, inner, gate, filt, skip, seg, wave, fwd, back)
 
 
 def distances(segment_ids):
@@ -398,19 +427,15 @@
     ids = lax.dynamic_slice_in_dim(jnp.concatenate([pad, segment_ids]), first, rows + HALO, 0)
     dist = lax.dynamic_slice_in_dim(jnp.concatenate([pad, distances(segment_ids)]), first, rows + HALO, 0)
     bounds = jnp.concatenate([ids[HALO::BLOCK], ids[HALO + BLOCK - 1 :: BLOCK]])
-    spread = lambda v: jnp.broadcast_to(v[:, None], (rows + HALO, 256))
+    spread = lambda v: jnp.broadcast_to(v[:, None], (rows + HALO, 128))
     forward, back = transforms()
-    full = jnp.dot(forward[:, : long_filter.shape[1]], long_filter.T, precision=lax.Precision.HIGHEST)
-    top = (jnp.arange(BLOCK) == 0)[:, None]
-    re, im = full[:BLOCK], full[BLOCK:]
-    spec = jnp.stack([re, jnp.where(top, 0.0, im), jnp.where(top, im, re)])
     last = jnp.zeros((1,), jnp.int32)
     n = rows // BLOCK
     bounds = jnp.concatenate([bounds[:n], last, bounds[n:]])
-    proj = project_all(nt, nc, tokens, in_weight, norm_gain[None, :])
+    inner, gate = project_all(nt, nc, tokens, in_weight, norm_gain[None, :], short_taps, spread(dist))
     return filter_gate(
-        proj, short_taps, spec, skip_bias[None, :], spread(dist), spread(ids), bounds,
-        jnp.asarray(forward, jnp.bfloat16), jnp.asarray(back, jnp.bfloat16),
+        inner, gate, long_filter, skip_bias[None, :], spread(ids), bounds,
+        jnp.asarray(forward[:, : long_filter.shape[1]]), jnp.asarray(forward, jnp.bfloat16), jnp.asarray(back, jnp.bfloat16),
     )
 
 

time: 247 us -> 191 us (0.77); the launches traced: 245 us -> 191 us
  Pallas kernels: 234 us -> 181 us
    pallas_call x1, Pallas kernels: 51.8 us -> 19.7 us  [filter_gate(): pl.pallas_call(conv_kernel, grid_spec=pltpu.PrefetchScalarGridSpec(num_sc...]
    pallas_call x1, Pallas kernels: 182 us -> 162 us  [project_all(): pl.pallas_call(functools.partial(gather_kernel, nt, nc), out_shape=(jax.S...]
where the time goes in v2:
time: 191 us
  Pallas kernels  181 us (95%)
  local copies, waits for them, and re-layouts  7.64 us (4%)
    pallas_call x1, Pallas kernels, project_all(): pl.pallas_call(functools.partial(gather_kernel, nt, nc), out_shape=(jax.S...  162 us
    pallas_call x1, Pallas kernels, filter_gate(): pl.pallas_call(conv_kernel, grid_spec=pltpu.PrefetchScalarGridSpec(num_sc...  19.7 us
    unnamed x14, local copies, waits for them, and re-layouts  4.02 us

profile of v2, /device:TPU:0, one launch (start us, length us, event | category | flops | bytes accessed | tf_op | source)
XLA Modules:
  0.0 191.1 jit_solution(13407625680233482272)
XLA Ops:
  0.0 1.2 slice.21
  1.8 0.9 select_bitcast_fusion
  2.7 0.3 reduce-window.9
  3.0 0.1 slice.25
  3.1 0.1 reduce-window.12
  3.1 0.1 slice_reduce_fusion
  3.3 0.1 bitcast_subtract_fusion
  3.3 0.8 pad_dynamic-slice_fusion
  4.1 0.1 slice.20
  4.2 0.1 slice.19
  4.3 0.1 pad_add_fusion.bounds
  4.4 0.2 broadcast_in_dim.26.seg
  4.6 1.0 broadcast_in_dim.24.dist
  5.7 0.0 copy-start.2
  5.7 0.0 copy-start.3
  5.7 0.0 copy-start.4
  5.7 0.0 copy-start.5
  5.7 0.0 copy-start.6
  5.7 161.6 %gather_project.1 = (bf16[1152,1024]{1,0:T(8,128)(2,1)}, f32[1152,1024]{1,0:T(8,128)}) custom-call(bf16[1024,1024]{1,0:T(8,128)(2,1)} %x_in.1, bf16[3,1024,1024]{2,1,0:T(8,128)(2,1)} %w_in.1, f32[1,4096]{1,0:T(1,128)} %bitcast.9, f32[3,7,1024]{2,1,0:T(8,128)} %taps.1, s32[1168,128]{1,0:T(8,128)} %broadcast_in_dim.24.dist), custom_call_target="tpu_custom_call" | custom-call | tf_op jit(solution)/shard_map/gather_project/pallas_call | solution.py:299
  167.3 0.0 copy-done.2
  167.3 0.0 copy-done.3
  167.3 0.0 copy-done.4
  167.3 0.0 copy-done.5
  167.3 0.0 copy-done.6
  167.3 0.0 copy-start
  167.4 2.3 %copy-done = f32[1152,1024]{1,0:T(8,128)S(1)} copy-done((f32[1152,1024]{1,0:T(8,128)S(1)}, f32[1152,1024]{1,0:T(8,128)}, u32[]{:S(2)}) %copy-start) | copy-done | bytes 4718616
  169.7 0.0 copy-start.1
  169.7 1.7 copy-done.1
  171.4 19.7 %filter_gate.1 = bf16[1024,1024]{1,0:T(8,128)(2,1)} custom-call(s32[17]{0:T(128)S(1)} %pad_add_fusion.bounds, bf16[1152,1024]{1,0:T(8,128)(2,1)S(1)} %copy-done.1, f32[1152,1024]{1,0:T(8,128)S(1)} %copy-done, f32[1024,128]{1,0:T(8,128)S(1)} %copy-done.2, f32[1,1024]{1,0:T(1,128)S(1)} %bitcast.7, s32[1168,128]{1,0:T(8,128)S(1)} %broadcast_in_dim.26.seg, ...), custom_call_target="tpu_custom_call" | custom-call | tf_op jit(solution)/shard_map/filter_gate/pallas_call | solution.py:391
Async XLA Ops:
  5.7 161.6 %copy-start.2 = (f32[1024,128]{1,0:T(8,128)S(1)}, f32[1024,128]{1,0:T(8,128)}, u32[]{:S(2)}) copy-start(f32[1024,128]{1,0:T(8,128)} %filt.1) | copy-start | bytes 1572868
  5.7 161.7 %copy-start.3 = (bf16[256,256]{1,0:T(8,128)(2,1)S(1)}, bf16[256,256]{1,0:T(8,128)(2,1)}, u32[]{:S(2)}) copy-start(bf16[256,256]{1,0:T(8,128)(2,1)} %constant.29.clone.fwd) | copy-start | bytes 393220
  5.7 161.7 %copy-start.4 = (f32[256,128]{1,0:T(8,128)S(1)}, f32[256,128]{1,0:T(8,128)}, u32[]{:S(2)}) copy-start(f32[256,128]{1,0:T(8,128)} %constant.28.clone.wave) | copy-start | bytes 393220
  5.7 161.7 %copy-start.5 = (bf16[128,256]{1,0:T(8,128)(2,1)S(1)}, bf16[128,256]{1,0:T(8,128)(2,1)}, u32[]{:S(2)}) copy-start(bf16[128,256]{1,0:T(8,128)(2,1)} %constant.30.clone.back) | copy-start | bytes 196612
  5.7 161.7 %copy-start.6 = (f32[1024]{0:T(1024)S(1)}, f32[1024]{0:T(1024)}, u32[]{:S(2)}) copy-start(f32[1024]{0:T(1024)} %param.15) | copy-start | bytes 12292
  167.3 2.3 %copy-start = (f32[1152,1024]{1,0:T(8,128)S(1)}, f32[1152,1024]{1,0:T(8,128)}, u32[]{:S(2)}) copy-start(f32[1152,1024]{1,0:T(8,128)} %get-tuple-element.8.gate) | copy-start | bytes 14155780
  169.7 1.7 copy-start.1

commit v3 on v2

--- a/solution.py
+++ b/solution.py
@@ -16,7 +16,7 @@
 POINTS = 256
 
 
-def gather_kernel(nt, nc, x_in, w_in, gain, taps, dist, inner, gate, xbuf, wbuf, normed, out, strip, loc, xs, xr, ys, yr, ps, pr, cs, cr, os_, or_, hs, hr):
+def gather_kernel(nt, nc, x_in, w_in, gain, taps, dist, inner_out, gate_out, xbuf, wbuf, normed, out, strip, inner, gate, flush, loc, xs, xr, ys, yr, ps, pr, cs, cr, os_, or_, hs, hr):
     d = lax.axis_index("dp")
     i = lax.axis_index("context")
     t = lax.axis_index("tensor")
@@ -163,7 +163,7 @@
                     ccopy(side, hop, g, 1, yb, c, 1 - d).start()
 
     steps = (nt - 2) * PIECES
-    cuts = (steps // 4, steps // 2, 3 * steps // 4)
+    cuts = (steps - 8, steps - 6, steps - 5)
     at = 0
     for g in range(3):
         lax.fori_loop(at, cuts[g], pass_x, 0)
@@ -171,7 +171,7 @@
         pass_w(g)
         if g:
             pass_p(g - 1)
-    lax.fori_loop(at, steps, pass_x, 0)
+    lax.fori_loop(at, steps - 4, pass_x, 0)
     pass_p(2)
 
     mine_x.wait()
@@ -214,6 +214,13 @@
         lax.fori_loop(0, 3 * (wide // tile), one, 0)
 
     ntaps = taps.shape[1]
+
+    def flushes(start):
+        at, k = pl.ds(start, BLOCK), start // BLOCK
+        return (
+            pltpu.make_async_copy(inner.at[at, :], inner_out.at[at, :], flush.at[0, k]),
+            pltpu.make_async_copy(gate.at[at, :], gate_out.at[at, :], flush.at[1, k]),
+        )
 
     def featurize(start):
         start = pl.multiple_of(start, BLOCK)
@@ -236,9 +243,16 @@
             return carry
 
         lax.fori_loop(0, wide // 128, column, 0)
+        for copy in flushes(start):
+            copy.start()
 
     def project_step(r, carry):
         project(r)
+        return carry
+
+    def pass_project(q, carry):
+        pass_x(steps - 4 + q, 0)
+        project(q)
         return carry
 
     def both(r, carry):
@@ -257,10 +271,10 @@
     def _():
         out[:, 0:HALO, :] = jnp.zeros((3, HALO, wide), jnp.bfloat16)
 
-    lax.fori_loop(0, 2, project_step, 0)
+    lax.fori_loop(0, 2, pass_project, 0)
     when(i < nc - 1, lambda: hcopy().start())
+    lax.fori_loop(2, 4, pass_project, 0)
     featurize(BLOCK + (PIECES - 1) * rows)
-    lax.fori_loop(2, 4, project_step, 0)
     when(i > 0, lambda: hcopy().wait_recv())
     featurize(0)
     featurize(BLOCK)
@@ -288,6 +302,13 @@
                     ccopy(side, hop, g, 1, yb, c, 1 - d).wait_send()
     ocopy(i).wait_send()
     when(i < nc - 1, lambda: hcopy().wait_send())
+
+    def flushed(k, carry):
+        for copy in flushes(pl.multiple_of(k * BLOCK, BLOCK)):
+            copy.wait()
+        return carry
+
+    lax.fori_loop(0, 1 + total_rows // BLOCK, flushed, 0)
 
 
 def project_all(nt, nc, tokens, in_weight, gain, taps, dist):
@@ -303,13 +324,16 @@
             jax.ShapeDtypeStruct((BLOCK + rows, wide), jnp.float32),
         ),
         in_specs=[pl.BlockSpec(memory_space=pl.ANY)] * 2 + [pl.BlockSpec(memory_space=pltpu.VMEM)] * 3,
-        out_specs=(pl.BlockSpec(memory_space=pltpu.VMEM),) * 2,
+        out_specs=(pl.BlockSpec(memory_space=pl.ANY),) * 2,
         scratch_shapes=[
             pltpu.VMEM((nt, rows, feats), jnp.bfloat16),
             pltpu.VMEM((3, nc * deep, wide), jnp.bfloat16),
             pltpu.VMEM((rows // PIECES, nt * feats), jnp.bfloat16),
             pltpu.VMEM((3, HALO + rows, wide), jnp.bfloat16),
             pltpu.VMEM((3, BLOCK + 16, 128), jnp.float32),
+            pltpu.VMEM((BLOCK + rows, wide), jnp.bfloat16),
+            pltpu.VMEM((BLOCK + rows, wide), jnp.float32),
+            dma((2, 1 + rows // BLOCK)),
             dma((2,)),
             dma((2, nt - 1, PIECES)),
             dma((2, nt - 1, PIECES)),
@@ -342,7 +366,7 @@
     return forward.astype(np.float32), back.astype(np.float32)
 
 
-def conv_kernel(bounds, inner, gate, filt, skip, seg, wave, fwd, back, out, spec):
+def conv_kernel(bounds, inner, gate, filt, skip, seg, lines, wave, fwd, back, out, spec):
     blocks = inner.shape[0] // BLOCK
     wide = out.shape[1]
     full = lax.dot_general(
@@ -353,36 +377,35 @@
     spec[0] = re0
     spec[1] = jnp.where(top, 0.0, im0)
     spec[2] = jnp.where(top, im0, re0)
-    f = fwd[...]
-    w = back[...]
     hb = POINTS // 2
 
     def filter_block(b, carry):
         start = pl.multiple_of(b * BLOCK, BLOCK)
-        window = inner[pl.ds(start, 2 * BLOCK), :].astype(jnp.float32)
-        ids = seg[pl.ds(pl.multiple_of(start + 16, 16), 2 * BLOCK), :]
-        ids = jnp.concatenate([ids] * (wide // 128), axis=1)
-        mine = ids[BLOCK:]
+        window = inner[pl.ds(start, 2 * BLOCK), :]
+        mine = seg[pl.ds(pl.multiple_of(start + 16 + BLOCK, 16), BLOCK), :]
+        mine = jnp.concatenate([mine] * (POINTS // 128), axis=1)
+        ids = lines[pl.ds(b, 1), :]
 
         def one(s, acc):
-            x = jnp.where(ids == s, window, 0.0).astype(jnp.bfloat16)
-            z = jnp.dot(f, x, preferred_element_type=jnp.float32)
+            f = jnp.where(ids == s, fwd[...], 0.0).astype(jnp.bfloat16)
+            w = jnp.where(mine == s, back[...], 0.0).astype(jnp.bfloat16)
+            z = jnp.dot(f, window, preferred_element_type=jnp.float32)
             a, bb = z[:hb], z[hb:]
             re = a * spec[0] - bb * spec[1]
             im = a * spec[1] + bb * spec[2]
             prod = jnp.concatenate([re, im], axis=0).astype(jnp.bfloat16)
-            return jnp.where(mine == s, jnp.dot(w, prod, preferred_element_type=jnp.float32), acc)
+            return acc + jnp.dot(w, prod, preferred_element_type=jnp.float32)
 
         conv = lax.fori_loop(bounds[b], bounds[blocks + b] + 1, one, jnp.zeros((BLOCK, out.shape[1]), jnp.float32))
         here = pl.ds(pl.multiple_of(start + BLOCK, BLOCK), BLOCK)
-        mixed = gate[here, :] * (conv + skip[...] * window[BLOCK:])
+        mixed = gate[here, :] * (conv + skip[...] * window[BLOCK:].astype(jnp.float32))
         out[pl.ds(start, BLOCK), :] = mixed.astype(jnp.bfloat16)
         return carry
 
     lax.fori_loop(0, blocks - 1, filter_block, 0)
 
 
-def filter_gate(inner, gate, filt, skip, seg, bounds, wave, fwd, back):
+def filter_gate(inner, gate, filt, skip, seg, lines, bounds, wave, fwd, back):
     ext, wide = inner.shape
     rows = ext - BLOCK
     cols = min(512, wide)
@@ -399,6 +422,7 @@
                 pl.BlockSpec((cols, filt.shape[1]), lambda j, b: (j, 0)),
                 column(1),
                 whole(seg),
+                whole(lines),
                 whole(wave),
                 whole(fwd),
                 whole(back),
@@ -409,7 +433,7 @@
         out_shape=jax.ShapeDtypeStruct((rows, wide), jnp.bfloat16),
         compiler_params=pltpu.CompilerParams(vmem_limit_bytes=40 << 20),
         name="filter_gate",
-    )(bounds, inner, gate, filt, skip, seg, wave, fwd, back)
+    )(bounds, inner, gate, filt, skip, seg, lines, wave, fwd, back)
 
 
 def distances(segment_ids):
@@ -429,13 +453,15 @@
     bounds = jnp.concatenate([ids[HALO::BLOCK], ids[HALO + BLOCK - 1 :: BLOCK]])
     spread = lambda v: jnp.broadcast_to(v[:, None], (rows + HALO, 128))
     forward, back = transforms()
+    near = lambda v: jnp.asarray(v.astype(jnp.bfloat16).astype(np.float32))
     last = jnp.zeros((1,), jnp.int32)
     n = rows // BLOCK
     bounds = jnp.concatenate([bounds[:n], last, bounds[n:]])
+    lines = jnp.stack([ids[16 + b * BLOCK : 16 + (b + 2) * BLOCK] for b in range(n)])
     inner, gate = project_all(nt, nc, tokens, in_weight, norm_gain[None, :], short_taps, spread(dist))
     return filter_gate(
-        inner, gate, long_filter, skip_bias[None, :], spread(ids), bounds,
-        jnp.asarray(forward[:, : long_filter.shape[1]]), jnp.asarray(forward, jnp.bfloat16), jnp.asarray(back, jnp.bfloat16),
+        inner, gate, long_filter, skip_bias[None, :], spread(ids), lines, bounds,
+        jnp.asarray(forward[:, : long_filter.shape[1]]), near(forward), near(back),
     )
 
 

time: 191 us -> 210 us (1.099)
  Pallas kernels: 181 us -> 198 us
    pallas_call x1, Pallas kernels: 162 us -> 178 us  [project_all(): pl.pallas_call(functools.partial(gather_kernel, nt, nc), out_shape=(jax.S...]
where the time goes in v3:
time: 210 us; the launch traced here: 209 us
  Pallas kernels  198 us (94%)
  local copies, waits for them, and re-layouts  8.79 us (4%)
    pallas_call x1, Pallas kernels, project_all(): pl.pallas_call(functools.partial(gather_kernel, nt, nc), out_shape=(jax.S...  178 us
    pallas_call x1, Pallas kernels, filter_gate(): pl.pallas_call(conv_kernel, grid_spec=pltpu.PrefetchScalarGridSpec(num_sc...  20.4 us

profile of v3, /device:TPU:0, one launch (start us, length us, event | category | flops | bytes accessed | tf_op | source)
XLA Modules:
  0.0 209.2 jit_solution(7271880659246264171)
XLA Ops:
  0.0 1.2 slice.45
  1.8 1.1 pad_dynamic-slice_fusion
  3.0 0.9 select_bitcast_fusion
  3.9 0.3 reduce-window.9
  4.2 0.1 slice.57
  4.2 0.1 reduce-window.12
  4.3 0.1 slice_reduce_fusion
  4.4 0.1 bitcast_subtract_fusion
  4.5 0.8 pad_dynamic-slice_fusion.8
  5.3 0.1 slice.44
  5.4 0.1 slice.43
  5.5 0.1 pad_add_fusion.bounds
  5.5 0.2 broadcast_in_dim.26.seg
  5.8 1.0 broadcast_in_dim.24.dist
  6.8 0.0 copy-start.2
  6.8 0.0 copy-start.3
  6.8 0.0 copy-start.4
  6.8 0.0 copy-start.5
  6.8 0.0 copy-start.6
  6.8 177.9 %gather_project.1 = (bf16[1152,1024]{1,0:T(8,128)(2,1)}, f32[1152,1024]{1,0:T(8,128)}) custom-call(bf16[1024,1024]{1,0:T(8,128)(2,1)} %x_in.1, bf16[3,1024,1024]{2,1,0:T(8,128)(2,1)} %w_in.1, f32[1,4096]{1,0:T(1,128)} %bitcast.17, f32[3,7,1024]{2,1,0:T(8,128)} %taps.1, s32[1168,128]{1,0:T(8,128)} %broadcast_in_dim.24.dist), custom_call_target="tpu_custom_call" | custom-call | tf_op jit(solution)/shard_map/gather_project/pallas_call | solution.py:320
  184.7 0.0 copy-done.2
  184.7 0.0 copy-done.3
  184.7 0.0 copy-done.4
  184.8 0.0 copy-done.5
  184.8 0.0 copy-done.6
  184.8 0.0 copy-start
  184.8 2.3 %copy-done = f32[1152,1024]{1,0:T(8,128)S(1)} copy-done((f32[1152,1024]{1,0:T(8,128)S(1)}, f32[1152,1024]{1,0:T(8,128)}, u32[]{:S(2)}) %copy-start) | copy-done | bytes 4718616
  187.1 0.0 copy-start.1
  187.1 1.7 copy-done.1
  188.8 20.4 %filter_gate.1 = bf16[1024,1024]{1,0:T(8,128)(2,1)} custom-call(s32[17]{0:T(128)S(1)} %pad_add_fusion.bounds, bf16[1152,1024]{1,0:T(8,128)(2,1)S(1)} %copy-done.1, f32[1152,1024]{1,0:T(8,128)S(1)} %copy-done, f32[1024,128]{1,0:T(8,128)S(1)} %copy-done.2, f32[1,1024]{1,0:T(1,128)S(1)} %bitcast.15, s32[1168,128]{1,0:T(8,128)S(1)} %broadcast_in_dim.26.seg, ...), custom_call_target="tpu_custom_call" | custom-call | tf_op jit(solution)/shard_map/filter_gate/pallas_call | solution.py:414
  (1 shorter events, 0.0 us)
Async XLA Ops:
  6.8 177.9 %copy-start.2 = (f32[1024,128]{1,0:T(8,128)S(1)}, f32[1024,128]{1,0:T(8,128)}, u32[]{:S(2)}) copy-start(f32[1024,128]{1,0:T(8,128)} %filt.1) | copy-start | bytes 1572868
  6.8 177.9 %copy-start.3 = (f32[256,256]{1,0:T(8,128)S(1)}, f32[256,256]{1,0:T(8,128)}, u32[]{:S(2)}) copy-start(f32[256,256]{1,0:T(8,128)} %constant.29.clone.fwd) | copy-start | bytes 786436
  6.8 177.9 %copy-start.4 = (f32[128,256]{1,0:T(8,128)S(1)}, f32[128,256]{1,0:T(8,128)}, u32[]{:S(2)}) copy-start(f32[128,256]{1,0:T(8,128)} %constant.30.clone.back) | copy-start | bytes 393220
  6.8 177.9 %copy-start.5 = (f32[256,128]{1,0:T(8,128)S(1)}, f32[256,128]{1,0:T(8,128)}, u32[]{:S(2)}) copy-start(f32[256,128]{1,0:T(8,128)} %constant.28.clone.wave) | copy-start | bytes 393220
  6.8 178.0 %copy-start.6 = (f32[1024]{0:T(1024)S(1)}, f32[1024]{0:T(1024)}, u32[]{:S(2)}) copy-start(f32[1024]{0:T(1024)} %param.15) | copy-start | bytes 12292
  184.8 2.3 %copy-start = (f32[1152,1024]{1,0:T(8,128)S(1)}, f32[1152,1024]{1,0:T(8,128)}, u32[]{:S(2)}) copy-start(f32[1152,1024]{1,0:T(8,128)} %get-tuple-element.8.gate) | copy-start | bytes 14155780
  187.1 1.7 copy-start.1

commit v4 on v2

--- a/solution.py
+++ b/solution.py
@@ -14,6 +14,7 @@
 HALO = 144
 BLOCK = 128
 POINTS = 256
+PARTS = 6
 
 
 def gather_kernel(nt, nc, x_in, w_in, gain, taps, dist, inner, gate, xbuf, wbuf, normed, out, strip, loc, xs, xr, ys, yr, ps, pr, cs, cr, os_, or_, hs, hr):
@@ -82,13 +83,18 @@
     def when(cond, f):
         pl.when(cond)(f)
 
+    def branch(g):
+        span = w_in.shape[2] // (PARTS // 3)
+        return g // (PARTS // 3), pl.ds(g % (PARTS // 3) * span, span)
+
     def wspan(block, part):
         return pl.ds(pl.multiple_of(block * deep + part * half, half), half)
 
     def ycopy(side, hop, g, yb, first):
         place = wspan(yb * 2 + c, d)
-        dst = wbuf.at[g, place, :]
-        src = w_in.at[g, pl.ds(pl.multiple_of(d * half, half), half), :] if first else dst
+        n, cols = branch(g)
+        dst = wbuf.at[n, place, cols]
+        src = w_in.at[n, pl.ds(pl.multiple_of(d * half, half), half), cols] if first else dst
         to = (d, i + 2, t) if side == 0 else (d, i - 2, t)
         return pltpu.make_async_remote_copy(src, dst, ys.at[side, hop, g], yr.at[side, hop, g], device_id=to, device_id_type=MESH)
 
@@ -105,11 +111,13 @@
         return y - 1 - hop if side == 0 else y + 1 + hop
 
     def pcopy(side, hop, g, yb, part):
-        at = wbuf.at[g, wspan(yb * 2 + c, part), :]
+        n, cols = branch(g)
+        at = wbuf.at[n, wspan(yb * 2 + c, part), cols]
         return pltpu.make_async_remote_copy(at, at, ps.at[side, hop, g], pr.at[side, hop, g], device_id=peer, device_id_type=MESH)
 
     def ccopy(side, hop, g, via, yb, core, part):
-        at = wbuf.at[g, wspan(yb * 2 + core, part), :]
+        n, cols = branch(g)
+        at = wbuf.at[n, wspan(yb * 2 + core, part), cols]
         return pltpu.make_async_remote_copy(at, at, cs.at[side, hop, g, via], cr.at[side, hop, g, via], device_id=sib, device_id_type=MESH)
 
     def ocopy(block):
@@ -118,7 +126,7 @@
 
     sides = (0, 1)
 
-    for g in range(3):
+    for g in range(PARTS):
         for side in sides:
             when(y_sends(side, 0), lambda: ycopy(side, 0, g, y, True).start())
 
@@ -163,21 +171,21 @@
                     ccopy(side, hop, g, 1, yb, c, 1 - d).start()
 
     steps = (nt - 2) * PIECES
-    cuts = (steps // 4, steps // 2, 3 * steps // 4)
+    cuts = [1 + (g + 1) * steps // (PARTS + 2) for g in range(PARTS)]
     at = 0
-    for g in range(3):
+    for g in range(PARTS):
         lax.fori_loop(at, cuts[g], pass_x, 0)
         at = cuts[g]
         pass_w(g)
         if g:
             pass_p(g - 1)
     lax.fori_loop(at, steps, pass_x, 0)
-    pass_p(2)
+    pass_p(PARTS - 1)
 
     mine_x.wait()
     mine_w.wait()
     ocopy(sib[1]).wait_recv()
-    for g in range(3):
+    for g in range(PARTS):
         for hop in range(ny - 1):
             for side in sides:
                 @pl.when(y_takes(side, hop))
@@ -275,7 +283,7 @@
         return carry
 
     lax.fori_loop(0, PIECES, drain, 0)
-    for g in range(3):
+    for g in range(PARTS):
         for hop in range(ny - 1):
             for side in sides:
                 when(y_sends(side, hop), lambda: ycopy(side, hop, g, y_sent(side, hop), False).wait_send())
@@ -313,12 +321,12 @@
             dma((2,)),
             dma((2, nt - 1, PIECES)),
             dma((2, nt - 1, PIECES)),
-            dma((2, hops, 3)),
-            dma((2, hops, 3)),
-            dma((2, hops, 3)),
-            dma((2, hops, 3)),
-            dma((2, hops, 3, 2)),
-            dma((2, hops, 3, 2)),
+            dma((2, hops, PARTS)),
+            dma((2, hops, PARTS)),
+            dma((2, hops, PARTS)),
+            dma((2, hops, PARTS)),
+            dma((2, hops, PARTS, 2)),
+            dma((2, hops, PARTS, 2)),
             dma,
             dma,
             dma,
@@ -407,7 +415,7 @@
             scratch_shapes=[pltpu.VMEM((3, BLOCK, cols), jnp.float32)],
         ),
         out_shape=jax.ShapeDtypeStruct((rows, wide), jnp.bfloat16),
-        compiler_params=pltpu.CompilerParams(vmem_limit_bytes=40 << 20),
+        compiler_params=pltpu.CompilerParams(vmem_limit_bytes=60 << 20),
         name="filter_gate",
     )(bounds, inner, gate, filt, skip, seg, wave, fwd, back)
 

time: 191 us -> 191 us (level)
  local copies, waits for them, and re-layouts: 7.64 us -> 4.43 us
  Pallas kernels: 181 us -> 183 us
    unnamed x14 -> x0, local copies, waits for them, and re-layouts: 4.02 us -> none
where the time goes in v4:
time: 191 us; the launch traced here: 190 us
  Pallas kernels  183 us (96%)
  local copies, waits for them, and re-layouts  4.43 us (2%)
    pallas_call x1, Pallas kernels, project_all(): pl.pallas_call(functools.partial(gather_kernel, nt, nc), out_shape=(jax.S...  162 us
    pallas_call x1, Pallas kernels, filter_gate(): pl.pallas_call(conv_kernel, grid_spec=pltpu.PrefetchScalarGridSpec(num_sc...  21.4 us

profile of v4, /device:TPU:0, one launch (start us, length us, event | category | flops | bytes accessed | tf_op | source)
XLA Modules:
  0.0 190.4 jit_solution(2089538637372545810)
XLA Ops:
  0.0 1.2 slice.21
  1.8 0.9 select_bitcast_fusion
  2.7 0.3 reduce-window.9
  3.0 0.1 slice.25
  3.1 0.1 reduce-window.12
  3.1 0.1 slice_reduce_fusion
  3.3 0.1 bitcast_subtract_fusion
  3.3 0.8 pad_dynamic-slice_fusion
  4.1 0.1 slice.20
  4.2 0.1 slice.19
  4.3 0.6 pad_add_fusion.bounds
  4.9 1.0 broadcast_in_dim.26.seg
  6.0 1.0 broadcast_in_dim.24.dist
  7.0 162.0 %gather_project.1 = (bf16[1152,1024]{1,0:T(8,128)(2,1)}, f32[1152,1024]{1,0:T(8,128)}) custom-call(bf16[1024,1024]{1,0:T(8,128)(2,1)} %x_in.1, bf16[3,1024,1024]{2,1,0:T(8,128)(2,1)} %w_in.1, f32[1,4096]{1,0:T(1,128)} %bitcast.8, f32[3,7,1024]{2,1,0:T(8,128)} %taps.1, s32[1168,128]{1,0:T(8,128)} %broadcast_in_dim.24.dist), custom_call_target="tpu_custom_call" | custom-call | tf_op jit(solution)/shard_map/gather_project/pallas_call | solution.py:307
  169.0 21.4 %filter_gate.1 = bf16[1024,1024]{1,0:T(8,128)(2,1)} custom-call(s32[17]{0:T(128)} %pad_add_fusion.bounds, bf16[1152,1024]{1,0:T(8,128)(2,1)} %get-tuple-element.7.inner, f32[1152,1024]{1,0:T(8,128)} %get-tuple-element.8.gate, f32[1024,128]{1,0:T(8,128)} %filt.1, f32[1,1024]{1,0:T(1,128)} %bitcast.9, s32[1168,128]{1,0:T(8,128)} %broadcast_in_dim.26.seg, ...), custom_call_target="tpu_custom_call" | custom-call | tf_op jit(solution)/shard_map/filter_gate/pallas_call | solution.py:399
